TPU v7x, 512 devices: a whole 4x4x16 slice. The times are simulated.
512 devices in a mesh: section: 8 (over x, core), expert: 8 (over z_lo), dp: 8 (over y, z_hi).
Axes of the slice: x: 4, y: 4, z: 16 (z_hi: 2, z_lo: 8; z = z_hi * 8 + z_lo), core: 2. Of those that a mesh axis runs over, the one named last changes fastest.
Arguments:
- layer_input: bfloat16 [8, 8192, 2048], P('section', ('expert', 'dp')), may hold values from -6 to 6
- output_grad: bfloat16 [8, 8192, 2048], P('section', ('expert', 'dp')), may hold values from -6 to 6
- expert_ids: int32 [8, 8192], P('section', ('expert', 'dp')), may hold values from 0 to 63, as said below
- w_gate: bfloat16 [8, 2048, 8192], P('section', None, ('expert', 'dp')), may hold values from -0.125 to 0.125
- w_up: bfloat16 [8, 2048, 8192], P('section', None, ('expert', 'dp')), may hold values from -0.125 to 0.125
- w_down: bfloat16 [8, 2048, 8192], P('section', None, ('expert', 'dp')), may hold values from -0.0625 to 0.0625
Outputs:
- input_grad: bfloat16 [8, 8192, 2048], P('section', ('expert', 'dp'))
- grad_gate: bfloat16 [8, 2048, 8192], P('section', None, ('expert', 'dp'))
- grad_up: bfloat16 [8, 2048, 8192], P('section', None, ('expert', 'dp'))
- grad_down: bfloat16 [8, 2048, 8192], P('section', None, ('expert', 'dp'))
Inputs may be any that keep to these rules, and one draw needn't show every extreme that they name: `expert_ids`: expert 0 is the expert of these weights. Every device's 128 tokens name expert 0 between 1 and 8 times, and on every section some device names it exactly 8 times.
All inputs are finite; a program needn't handle non-finite values.
Results may differ from a plain program's by a relative error of at most 0.0065.
Values may be sent and summed in bfloat16 or wider, within the bound.
A program may use at most 64 MiB of HBM per device.

v0:
```python
import jax
import jax.numpy as jnp
from jax import lax
from jax.sharding import PartitionSpec as P

SLOT = 8


def shifted(value, axis, steps):
    count = lax.axis_size(axis)
    pairs = [(source, (source + steps) % count) for source in range(count)]
    return lax.ppermute(value, axis, pairs)


def unit_grads(x_rows, dy_rows, w_gate, w_up, w_down):
    gate = jnp.dot(x_rows, w_gate, preferred_element_type=jnp.float32)
    upper = jnp.dot(x_rows, w_up, preferred_element_type=jnp.float32)
    sigma = jax.nn.sigmoid(gate)
    active = gate * sigma
    hidden = (active * upper).astype(jnp.bfloat16)
    d_hidden = jnp.dot(dy_rows, w_down, preferred_element_type=jnp.float32)
    d_gate = (d_hidden * upper * sigma * (1.0 + gate * (1.0 - sigma))).astype(jnp.bfloat16)
    d_up = (d_hidden * active).astype(jnp.bfloat16)
    back_dims = (((1,), (1,)), ((), ()))
    d_input = lax.dot_general(d_gate, w_gate, back_dims, preferred_element_type=jnp.float32)
    d_input = d_input + lax.dot_general(d_up, w_up, back_dims, preferred_element_type=jnp.float32)
    return (d_input, d_gate, d_up, hidden)


def weight_grads(x_rows, dy_rows, d_gate, d_up, hidden):
    row_dims = (((0,), (0,)), ((), ()))
    part_gate = lax.dot_general(x_rows, d_gate, row_dims, preferred_element_type=jnp.float32)
    part_up = lax.dot_general(x_rows, d_up, row_dims, preferred_element_type=jnp.float32)
    part_down = lax.dot_general(dy_rows, hidden, row_dims, preferred_element_type=jnp.float32)
    return (part_gate, part_up, part_down)


def body(layer_input, output_grad, expert_ids, w_gate, w_up, w_down):
    inputs = layer_input[0]
    grads = output_grad[0]
    routes = expert_ids[0]
    chosen = (routes == 0).astype(jnp.int32)
    order = jnp.arange(chosen.shape[0], dtype=jnp.int32)
    within = jnp.sum(jnp.where(order[None, :] < order[:, None], chosen[None, :], 0), axis=1)
    target = jnp.where(chosen > 0, within, SLOT)
    places = jnp.arange(SLOT, dtype=jnp.int32)
    match = (target[None, :] == places[:, None]).astype(jnp.bfloat16)
    send_x = jnp.dot(match, inputs, preferred_element_type=jnp.float32).astype(jnp.bfloat16)
    send_dy = jnp.dot(match, grads, preferred_element_type=jnp.float32).astype(jnp.bfloat16)
    group_x, group_dy = (
        lax.all_gather(send_x, "expert", axis=0, tiled=True),
        lax.all_gather(send_dy, "expert", axis=0, tiled=True),
    )
    full_gate, full_up, full_down = (
        lax.all_gather(w_gate[0], "dp", axis=1, tiled=True),
        lax.all_gather(w_up[0], "dp", axis=1, tiled=True),
        lax.all_gather(w_down[0], "dp", axis=1, tiled=True),
    )
    d_part, d_gate, d_up, hidden = unit_grads(group_x, group_dy, full_gate, full_up, full_down)
    mine = lax.psum_scatter(d_part.astype(jnp.bfloat16), "expert", scatter_dimension=0, tiled=True)
    own_gate, own_up, own_hidden = (
        lax.all_to_all(d_gate, "dp", split_axis=1, concat_axis=0, tiled=True),
        lax.all_to_all(d_up, "dp", split_axis=1, concat_axis=0, tiled=True),
        lax.all_to_all(hidden, "dp", split_axis=1, concat_axis=0, tiled=True),
    )
    every_x, every_dy = (
        lax.all_gather(group_x, "dp", axis=0, tiled=True),
        lax.all_gather(group_dy, "dp", axis=0, tiled=True),
    )
    part_gate, part_up, part_down = weight_grads(every_x, every_dy, own_gate, own_up, own_hidden)
    d_rows = lax.optimization_barrier(mine)
    term = lax.dot_general(
        match, d_rows, (((0,), (0,)), ((), ())), preferred_element_type=jnp.float32
    )
    token_grad = (grads.astype(jnp.float32) + term).astype(jnp.bfloat16)
    moved = shifted(token_grad, "section", -1)
    return (
        moved[None],
        part_gate.astype(jnp.bfloat16)[None],
        part_up.astype(jnp.bfloat16)[None],
        part_down.astype(jnp.bfloat16)[None],
    )


def solution(mesh):
    in_specs = (
        P("section", ("expert", "dp"), None),
        P("section", ("expert", "dp"), None),
        P("section", ("expert", "dp")),
        P("section", None, ("expert", "dp")),
        P("section", None, ("expert", "dp")),
        P("section", None, ("expert", "dp")),
    )
    out_specs = (
        P("section", ("expert", "dp"), None),
        P("section", None, ("expert", "dp")),
        P("section", None, ("expert", "dp")),
        P("section", None, ("expert", "dp")),
    )
    return jax.shard_map(body, mesh=mesh, in_specs=in_specs, out_specs=out_specs, check_vma=False)
```

profile of v0, /device:TPU:16, one launch (start us, length us, event | category | flops | bytes accessed | tf_op | source)
XLA Modules:
  0.0 865.1 jit_solution(10704545008492486408)
XLA Ops:
  7.2 0.7 all-gather.17.cloned.1.call-update
  8.0 0.7 all-gather.15.cloned.1.call-update
  8.7 0.7 all-gather.13.cloned.1.call-update
  9.4 0.7 fusion.28
  10.2 0.7 fusion.27
  11.1 57.3 %all_gather.23 = bf16[64,2048]{1,0:T(8,128)(2,1)S(1)} all-gather(bf16[8,2048]{1,0:T(8,128)(2,1)S(1)} %convolution_convert_fusion.3), channel_id=1, replica_groups=mesh['section'=8,'expert'=8,'dp'=8] {'expert'}, dimensions={0}, use_global_device_ids=true | all-gather | bytes 294912 | tf_op jit(solution)/shard_map/all_gather | solution.py:51
  68.4 1.3 convolution_convert_fusion.4
  69.7 84.0 %all_gather.21 = bf16[64,2048]{1,0:T(8,128)(2,1)S(1)} all-gather(bf16[8,2048]{1,0:T(8,128)(2,1)S(1)} %convolution_convert_fusion.4), channel_id=1, replica_groups=mesh['section'=8,'expert'=8,'dp'=8] {'expert'}, dimensions={0}, use_global_device_ids=true | all-gather | bytes 294912 | tf_op jit(solution)/shard_map/all_gather | solution.py:52
  153.8 48.7 %all-gather.17.cloned.1.call-done = bf16[1,2048,1024]{2,1,0:T(8,128)(2,1)} async-done(((bf16[1,2048,128]{2,1,0:T(8,128)(2,1)}), bf16[1,2048,1024]{2,1,0:T(8,128)(2,1)}) %all-gather.17.cloned.1.call-update) | async-done | bytes 4194320 | tf_op jit(solution)/shard_map/all_gather | solution.py:55
  202.5 3.0 fusion.2
  205.5 174.7 %all-gather.15.cloned.1.call-done = bf16[1,2048,1024]{2,1,0:T(8,128)(2,1)} async-done(((bf16[1,2048,128]{2,1,0:T(8,128)(2,1)}), bf16[1,2048,1024]{2,1,0:T(8,128)(2,1)}) %all-gather.15.cloned.1.call-update) | async-done | bytes 4194320 | tf_op jit(solution)/shard_map/all_gather | solution.py:56
  380.2 3.0 fusion.6
  383.2 175.2 %all-gather.13.cloned.1.call-done = bf16[1,2048,1024]{2,1,0:T(8,128)(2,1)} async-done(((bf16[1,2048,128]{2,1,0:T(8,128)(2,1)}), bf16[1,2048,1024]{2,1,0:T(8,128)(2,1)}) %all-gather.13.cloned.1.call-update) | async-done | bytes 4194320 | tf_op jit(solution)/shard_map/all_gather | solution.py:57
  558.4 3.2 fusion.23
  561.8 1.4 fusion
  563.2 2.1 fusion.17
  565.4 0.5 all-gather.9.cloned.1.call-update
  566.5 0.7 copy_bitcast_fusion.2
  567.2 5.7 all-to-all-start
  572.9 0.7 copy_bitcast_fusion.1
  573.6 12.6 %all-to-all-done = bf16[64,8,128]{2,0,1:T(8,128)(2,1)S(1)} async-done(((bf16[64,8,128]{2,0,1:T(8,128)(2,1)}), bf16[64,8,128]{2,0,1:T(8,128)(2,1)S(1)}, u32[]{:S(2)}, u32[]{:S(2)}) %all-to-all-start) | async-done | bytes 131104 | tf_op jit(solution)/shard_map/all_to_all | solution.py:62
  586.3 5.8 all-to-all-start.1
  592.0 0.7 copy.22
  592.7 30.8 %reduce-scatter.2.cloned.1.call-done = bf16[8,2048]{1,0:T(8,128)(2,1)} async-done(((bf16[64,2048]{1,0:T(8,128)(2,1)}), bf16[8,2048]{1,0:T(8,128)(2,1)}) %reduce-scatter.2.cloned.1.call-update) | async-done | bytes 32784 | tf_op jit(solution)/shard_map/reduce_scatter | solution.py:60
  623.5 6.7 all-to-all-start.2
  630.2 1.1 fusion.10
  631.3 107.6 %all-gather.9.cloned.1.call-done = bf16[512,2048]{1,0:T(8,128)(2,1)} async-done(((bf16[64,2048]{1,0:T(8,128)(2,1)}), bf16[512,2048]{1,0:T(8,128)(2,1)}) %all-gather.9.cloned.1.call-update) | async-done | bytes 2097168 | tf_op jit(solution)/shard_map/all_gather | solution.py:67
  738.9 3.3 fusion.14
  742.2 1.6 fusion.15
  743.8 110.6 %all-gather.11.cloned.1.call-done = bf16[512,2048]{1,0:T(8,128)(2,1)} async-done(((bf16[64,2048]{1,0:T(8,128)(2,1)}), bf16[512,2048]{1,0:T(8,128)(2,1)}) %all-gather.11.cloned.1.call-update) | async-done | bytes 2097168 | tf_op jit(solution)/shard_map/all_gather | solution.py:68
  854.4 3.1 fusion.16
  857.5 0.8 copy.24
  (28 shorter events, 1.3 us)
Async XLA Ops:
  7.2 3.7 copy-start
  7.2 195.3 %all-gather.17.cloned.1.call-start = ((), (), s32[]{:S(2)}) async-start(), calls=%async_computation.9 | async-start | bytes 4718592 | tf_op jit(solution)/shard_map/all_gather | solution.py:55
  7.9 372.2 %all-gather.15.cloned.1.call-start = ((), (), s32[]{:S(2)}) async-start(), calls=%async_computation.8 | async-start | bytes 4718592 | tf_op jit(solution)/shard_map/all_gather | solution.py:56
  8.7 549.7 %all-gather.13.cloned.1.call-start = ((), (), s32[]{:S(2)}) async-start(), calls=%async_computation.7 | async-start | bytes 4718592 | tf_op jit(solution)/shard_map/all_gather | solution.py:57
  9.4 614.1 %reduce-scatter.2.cloned.1.call-start = ((), (), s32[]{:S(2)}) async-start(), calls=%async_computation.4 | async-start | bytes 294912 | tf_op jit(solution)/shard_map/reduce_scatter | solution.py:60
  68.4 314.8 %copy-start.4 = (bf16[64,2048]{1,0:T(8,128)(2,1)}, bf16[64,2048]{1,0:T(8,128)(2,1)S(1)}, u32[]{:S(2)}) copy-start(bf16[64,2048]{1,0:T(8,128)(2,1)S(1)} %all_gather.23) | copy-start | bytes 786436
  153.8 404.6 %copy-start.5 = (bf16[64,2048]{1,0:T(8,128)(2,1)}, bf16[64,2048]{1,0:T(8,128)(2,1)S(1)}, u32[]{:S(2)}) copy-start(bf16[64,2048]{1,0:T(8,128)(2,1)S(1)} %all_gather.21) | copy-start | bytes 786436
  558.4 3.4 copy-start.2
  558.4 4.8 copy-start.3
  563.2 67.0 %copy-start.6 = (bf16[1,128,2048]{2,1,0:T(8,128)(2,1)S(1)}, bf16[1,128,2048]{2,1,0:T(8,128)(2,1)}, u32[]{:S(2)}) copy-start(bf16[1,128,2048]{2,1,0:T(8,128)(2,1)} %param.7) | copy-start | bytes 1572868
  565.4 173.6 %all-gather.9.cloned.1.call-start = ((), (), s32[]{:S(2)}) async-start(), calls=%async_computation.5 | async-start | bytes 2359296 | tf_op jit(solution)/shard_map/all_gather | solution.py:67
  565.9 288.4 %all-gather.11.cloned.1.call-start = ((), (), s32[]{:S(2)}) async-start(), calls=%async_computation.6 | async-start | bytes 2359296 | tf_op jit(solution)/shard_map/all_gather | solution.py:68
  567.2 19.1 %all-to-all-start = ((bf16[64,8,128]{2,0,1:T(8,128)(2,1)}), bf16[64,8,128]{2,0,1:T(8,128)(2,1)S(1)}, u32[]{:S(2)}, u32[]{:S(2)}) async-start(bf16[64,8,128]{2,0,1:T(8,128)(2,1)} %copy_bitcast_fusion.2), calls=%async_computation.1 | async-start | bytes 262144 | tf_op jit(solution)/shard_map/all_to_all | solution.py:62
  586.3 37.2 %all-to-all-start.1 = ((bf16[64,8,128]{2,0,1:T(8,128)(2,1)}), bf16[64,8,128]{2,0,1:T(8,128)(2,1)S(1)}, u32[]{:S(2)}, u32[]{:S(2)}) async-start(bf16[64,8,128]{2,0,1:T(8,128)(2,1)} %copy_bitcast_fusion.1), calls=%async_computation.2 | async-start | bytes 262144 | tf_op jit(solution)/shard_map/all_to_all | solution.py:63
  623.5 230.9 %all-to-all-start.2 = ((bf16[64,8,128]{2,0,1:T(8,128)(2,1)}), bf16[64,8,128]{2,0,1:T(8,128)(2,1)S(1)}, u32[]{:S(2)}, u32[]{:S(2)}) async-start(bf16[64,8,128]{2,0,1:T(8,128)(2,1)} %bitcast.74), calls=%async_computation.3 | async-start | bytes 262144 | tf_op jit(solution)/shard_map/all_to_all | solution.py:64
  631.3 226.2 %collective-permute-start = (bf16[128,2048]{1,0:T(8,128)(2,1)S(1)}, bf16[128,2048]{1,0:T(8,128)(2,1)S(1)}, u32[]{:S(2)}, u32[]{:S(2)}) collective-permute-start(bf16[128,2048]{1,0:T(8,128)(2,1)S(1)} %fusion.10), channel_id=1, source_target_pairs={{0,448},{64,0},{128,64},{192,128},{256,192},{320,256},{384,320},{4... | collective-permute-start | bytes 1572872 | tf_op jit(solution)/shard_map/ppermute | solution.py:12
  738.9 3.3 copy-start.1
Sparse Core Ops, SparseCore 0:
  11.1 191.3 all-gather.16
  205.5 174.5 all-gather.14
  383.2 175.0 all-gather.12
  565.5 57.9 reduce-scatter.1
  627.6 111.2 all-gather.8
  743.0 111.2 all-gather.10
where the time goes:
time: 866 us; the launch traced here: 865 us
  waiting for transfers between devices  663 us (77%)
  blocking collectives  141 us (16%)
  matrix products  23.4 us (3%)
  starting transfers between devices  18.5 us (2%)
  between operations  14.2 us (2%)
    all_gather x1, waiting for transfers between devices, body(): lax.all_gather(w_down[0], 'dp', axis=1, tiled=True)  175 us
    all_gather x1, waiting for transfers between devices, body(): lax.all_gather(w_up[0], 'dp', axis=1, tiled=True)  175 us
    all_gather x1, waiting for transfers between devices, body(): lax.all_gather(group_dy, 'dp', axis=0, tiled=True)  111 us
    all_gather x1, waiting for transfers between devices, body(): lax.all_gather(group_x, 'dp', axis=0, tiled=True)  108 us
    all_gather x1, blocking collectives, body(): lax.all_gather(send_dy, 'expert', axis=0, tiled=True)  84 us
    all_gather x1, blocking collectives, body(): lax.all_gather(send_x, 'expert', axis=0, tiled=True)  57.3 us
    all_gather x1, waiting for transfers between devices, body(): lax.all_gather(w_gate[0], 'dp', axis=1, tiled=True)  48.7 us
    reduce_scatter x1, waiting for transfers between devices, body(): lax.psum_scatter(d_part.astype(jnp.bfloat16), 'expert', scatter_dimension...  30.8 us
  transfers between devices with their start and end apart: 10, of which 7 were waited for; matrix products, arithmetic and copies ran while one was open for 2% of the time, Pallas kernels for 0%

commit v1 on v0

--- a/solution.py
+++ b/solution.py
@@ -4,6 +4,11 @@
 from jax.sharding import PartitionSpec as P
 
 SLOT = 8
+
+
+def swapped_in(shard, axis, dim):
+    sent = jnp.stack([shard] * lax.axis_size(axis))
+    return jnp.concatenate(lax.all_to_all(sent, axis, 0, 0), axis=dim)
 
 
 def shifted(value, axis, steps):
@@ -64,7 +69,7 @@
         lax.all_to_all(hidden, "dp", split_axis=1, concat_axis=0, tiled=True),
     )
     every_x, every_dy = (
-        lax.all_gather(group_x, "dp", axis=0, tiled=True),
+        swapped_in(group_x, "dp", 0),
         lax.all_gather(group_dy, "dp", axis=0, tiled=True),
     )
     part_gate, part_up, part_down = weight_grads(every_x, every_dy, own_gate, own_up, own_hidden)

time: 866 us -> 838 us (0.968)
  waiting for transfers between devices: 663 us -> 490 us
  blocking collectives: 141 us -> 266 us
  starting transfers between devices: 18.5 us -> 37.1 us
    all_gather x1, blocking collectives: 84 us -> 209 us  [body(): lax.all_gather(send_dy, 'expert', axis=0, tiled=True)]
    all_gather x1 -> x0, waiting for transfers between devices: 108 us -> none  [body(): lax.all_gather(group_x, 'dp', axis=0, tiled=True)]
    all_gather x1, waiting for transfers between devices: 48.7 us -> 0.01 us  [body(): lax.all_gather(w_gate[0], 'dp', axis=1, tiled=True)]
    all_to_all x0 -> x1, starting transfers between devices: none -> 17.2 us  [swapped_in(): return jnp.concatenate(lax.all_to_all(sent, axis, 0, 0), axis=dim)]
    all_to_all x1, waiting for transfers between devices: 0.01 us -> 12.7 us  [body(): lax.all_to_all(d_up, 'dp', split_axis=1, concat_axis=0, tiled=True)]
    all_to_all x1, waiting for transfers between devices: 12.6 us -> 0.01 us  [body(): lax.all_to_all(d_gate, 'dp', split_axis=1, concat_axis=0, tiled=True)]
    all_gather x1, waiting for transfers between devices: 175 us -> 163 us  [body(): lax.all_gather(w_up[0], 'dp', axis=1, tiled=True)]
  transfers between devices with their start and end apart: 10 -> 10, of which waited for: 7 -> 5; matrix products, arithmetic and copies ran while one was open for 2% -> 3% of each run, Pallas kernels for 0% -> 0%
where the time goes in v1:
time: 838 us; the launch traced here: 837 us
  waiting for transfers between devices  490 us (58%)
  blocking collectives  266 us (32%)
  starting transfers between devices  37.1 us (4%)
  matrix products  23.1 us (3%)
  between operations  13.8 us (2%)
    all_gather x1, blocking collectives, body(): lax.all_gather(send_dy, 'expert', axis=0, tiled=True)  209 us
    all_gather x1, waiting for transfers between devices, body(): lax.all_gather(w_down[0], 'dp', axis=1, tiled=True)  174 us
    all_gather x1, waiting for transfers between devices, body(): lax.all_gather(w_up[0], 'dp', axis=1, tiled=True)  163 us
    all_gather x1, waiting for transfers between devices, body(): lax.all_gather(group_dy, 'dp', axis=0, tiled=True)  107 us
    all_gather x1, blocking collectives, body(): lax.all_gather(send_x, 'expert', axis=0, tiled=True)  57.2 us
    reduce_scatter x1, waiting for transfers between devices, body(): lax.psum_scatter(d_part.astype(jnp.bfloat16), 'expert', scatter_dimension...  30.5 us
    all_to_all x1, starting transfers between devices, swapped_in(): return jnp.concatenate(lax.all_to_all(sent, axis, 0, 0), axis=dim)  17.2 us
  transfers between devices with their start and end apart: 10, of which 5 were waited for; matrix products, arithmetic and copies ran while one was open for 3% of the time, Pallas kernels for 0%

profile of v1, /device:TPU:16, one launch (start us, length us, event | category | flops | bytes accessed | tf_op | source)
XLA Modules:
  0.0 837.2 jit_solution(6762897580968210608)
XLA Ops:
  7.2 0.7 all-gather.14.cloned.1.call-update
  8.0 0.7 all-gather.12.cloned.1.call-update
  8.7 0.7 all-gather.10.cloned.1.call-update
  9.4 0.7 fusion.32
  10.2 0.7 fusion.31
  11.0 57.2 %all_gather.20 = bf16[64,2048]{1,0:T(8,128)(2,1)S(1)} all-gather(bf16[8,2048]{1,0:T(8,128)(2,1)S(1)} %convolution_convert_fusion.1), channel_id=1, replica_groups=mesh['section'=8,'expert'=8,'dp'=8] {'expert'}, dimensions={0}, use_global_device_ids=true | all-gather | bytes 294912 | tf_op jit(solution)/shard_map/all_gather | solution.py:56
  68.3 1.6 stack.2
  69.8 17.2 %all-to-all-start = ((bf16[8,64,2048]{2,1,0:T(8,128)(2,1)}), bf16[8,64,2048]{2,1,0:T(8,128)(2,1)S(1)}, u32[]{:S(2)}, u32[]{:S(2)}) async-start(bf16[8,64,2048]{2,1,0:T(8,128)(2,1)} %stack.2), calls=%async_computation.1 | async-start | bytes 4194304 | tf_op jit(solution)/shard_map/all_to_all | solution.py:11
  87.2 209.1 %all_gather.18 = bf16[64,2048]{1,0:T(8,128)(2,1)S(1)} all-gather(bf16[8,2048]{1,0:T(8,128)(2,1)S(1)} %convolution_convert_fusion.2), channel_id=1, replica_groups=mesh['section'=8,'expert'=8,'dp'=8] {'expert'}, dimensions={0}, use_global_device_ids=true | all-gather | bytes 294912 | tf_op jit(solution)/shard_map/all_gather | solution.py:57
  296.4 4.0 fusion.2
  300.4 162.6 %all-gather.12.cloned.1.call-done = bf16[1,2048,1024]{2,1,0:T(8,128)(2,1)} async-done(((bf16[1,2048,128]{2,1,0:T(8,128)(2,1)}), bf16[1,2048,1024]{2,1,0:T(8,128)(2,1)}) %all-gather.12.cloned.1.call-update) | async-done | bytes 4194320 | tf_op jit(solution)/shard_map/all_gather | solution.py:61
  463.0 3.7 fusion.6
  466.8 174.5 %all-gather.10.cloned.1.call-done = bf16[1,2048,1024]{2,1,0:T(8,128)(2,1)} async-done(((bf16[1,2048,128]{2,1,0:T(8,128)(2,1)}), bf16[1,2048,1024]{2,1,0:T(8,128)(2,1)}) %all-gather.10.cloned.1.call-update) | async-done | bytes 4194320 | tf_op jit(solution)/shard_map/all_gather | solution.py:62
  641.2 3.4 fusion.25
  644.8 1.4 fusion
  646.2 2.1 fusion.19
  648.4 0.5 all-gather.8.cloned.1.call-update
  649.0 0.7 copy_bitcast_fusion.1
  649.6 5.7 all-to-all-start.2
  655.4 0.7 copy.24
  656.1 12.7 %all-to-all-done.2 = bf16[64,8,128]{2,0,1:T(8,128)(2,1)S(1)} async-done(((bf16[64,8,128]{2,0,1:T(8,128)(2,1)}), bf16[64,8,128]{2,0,1:T(8,128)(2,1)S(1)}, u32[]{:S(2)}, u32[]{:S(2)}) %all-to-all-start.2) | async-done | bytes 131104 | tf_op jit(solution)/shard_map/all_to_all | solution.py:68
  668.8 0.7 copy-done.6
  669.4 5.9 all-to-all-start.3
  675.4 0.7 copy_bitcast_fusion.2
  676.0 30.5 %reduce-scatter.2.cloned.1.call-done = bf16[8,2048]{1,0:T(8,128)(2,1)} async-done(((bf16[64,2048]{1,0:T(8,128)(2,1)}), bf16[8,2048]{1,0:T(8,128)(2,1)}) %reduce-scatter.2.cloned.1.call-update) | async-done | bytes 32784 | tf_op jit(solution)/shard_map/reduce_scatter | solution.py:65
  706.5 1.9 fusion.12
  708.4 8.0 all-to-all-start.1
  716.4 107.1 %all-gather.8.cloned.1.call-done = bf16[512,2048]{1,0:T(8,128)(2,1)} async-done(((bf16[64,2048]{1,0:T(8,128)(2,1)}), bf16[512,2048]{1,0:T(8,128)(2,1)}) %all-gather.8.cloned.1.call-update) | async-done | bytes 2097168 | tf_op jit(solution)/shard_map/all_gather | solution.py:73
  823.6 3.1 fusion.16
  826.7 1.6 fusion.17
  828.3 1.6 fusion.18
  829.8 0.8 copy.26
  (30 shorter events, 0.9 us)
Async XLA Ops:
  7.2 3.7 copy-start
  7.2 289.2 %all-gather.14.cloned.1.call-start = ((), (), s32[]{:S(2)}) async-start(), calls=%async_computation.9 | async-start | bytes 4718592 | tf_op jit(solution)/shard_map/all_gather | solution.py:60
  7.9 79.1 %copy-start.4 = (bf16[1,128,2048]{2,1,0:T(8,128)(2,1)S(1)}, bf16[1,128,2048]{2,1,0:T(8,128)(2,1)}, u32[]{:S(2)}) copy-start(bf16[1,128,2048]{2,1,0:T(8,128)(2,1)} %param.7) | copy-start | bytes 1572868
  7.9 455.1 %all-gather.12.cloned.1.call-start = ((), (), s32[]{:S(2)}) async-start(), calls=%async_computation.8 | async-start | bytes 4718592 | tf_op jit(solution)/shard_map/all_gather | solution.py:61
  8.7 632.6 %all-gather.10.cloned.1.call-start = ((), (), s32[]{:S(2)}) async-start(), calls=%async_computation.7 | async-start | bytes 4718592 | tf_op jit(solution)/shard_map/all_gather | solution.py:62
  69.8 579.8 %all-to-all-start = ((bf16[8,64,2048]{2,1,0:T(8,128)(2,1)}), bf16[8,64,2048]{2,1,0:T(8,128)(2,1)S(1)}, u32[]{:S(2)}, u32[]{:S(2)}) async-start(bf16[8,64,2048]{2,1,0:T(8,128)(2,1)} %stack.2), calls=%async_computation.1 | async-start | bytes 4194304 | tf_op jit(solution)/shard_map/all_to_all | solution.py:11
  87.1 619.5 %reduce-scatter.2.cloned.1.call-start = ((), (), s32[]{:S(2)}) async-start(), calls=%async_computation.5 | async-start | bytes 294912 | tf_op jit(solution)/shard_map/reduce_scatter | solution.py:65
  296.4 344.9 %copy-start.3 = (bf16[64,2048]{1,0:T(8,128)(2,1)}, bf16[64,2048]{1,0:T(8,128)(2,1)S(1)}, u32[]{:S(2)}) copy-start(bf16[64,2048]{1,0:T(8,128)(2,1)S(1)} %all_gather.18) | copy-start | bytes 786436
  641.2 3.6 copy-start.1
  641.2 5.0 copy-start.2
  646.2 60.3 %copy-start.5 = (bf16[1,128,2048]{2,1,0:T(8,128)(2,1)S(1)}, bf16[1,128,2048]{2,1,0:T(8,128)(2,1)}, u32[]{:S(2)}) copy-start(bf16[1,128,2048]{2,1,0:T(8,128)(2,1)} %param.7) | copy-start | bytes 1572868
  648.4 175.2 %all-gather.8.cloned.1.call-start = ((), (), s32[]{:S(2)}) async-start(), calls=%async_computation.6 | async-start | bytes 2359296 | tf_op jit(solution)/shard_map/all_gather | solution.py:73
  649.6 19.1 %all-to-all-start.2 = ((bf16[64,8,128]{2,0,1:T(8,128)(2,1)}), bf16[64,8,128]{2,0,1:T(8,128)(2,1)S(1)}, u32[]{:S(2)}, u32[]{:S(2)}) async-start(bf16[64,8,128]{2,0,1:T(8,128)(2,1)} %copy_bitcast_fusion.1), calls=%async_computation.3 | async-start | bytes 262144 | tf_op jit(solution)/shard_map/all_to_all | solution.py:68
  668.8 0.7 copy-start.6
  669.4 39.0 %all-to-all-start.3 = ((bf16[64,8,128]{2,0,1:T(8,128)(2,1)}), bf16[64,8,128]{2,0,1:T(8,128)(2,1)S(1)}, u32[]{:S(2)}, u32[]{:S(2)}) async-start(bf16[64,8,128]{2,0,1:T(8,128)(2,1)} %bitcast.84), calls=%async_computation.4 | async-start | bytes 262144 | tf_op jit(solution)/shard_map/all_to_all | solution.py:69
  675.4 151.4 %copy-start.7 = (bf16[64,8,128]{2,0,1:T(8,128)(2,1)S(1)}, bf16[64,8,128]{2,0,1:T(8,128)(2,1)}, u32[]{:S(2)}) copy-start(bf16[64,8,128]{2,0,1:T(8,128)(2,1)} %copy-done.6) | copy-start | bytes 393220
  708.4 121.4 %collective-permute-start = (bf16[128,2048]{1,0:T(8,128)(2,1)}, bf16[128,2048]{1,0:T(8,128)(2,1)S(1)}, u32[]{:S(2)}, u32[]{:S(2)}) collective-permute-start(bf16[128,2048]{1,0:T(8,128)(2,1)} %fusion.12), channel_id=1, source_target_pairs={{0,448},{64,0},{128,64},{192,128},{256,192},{320,256},{384,320},{4... | collective-permute-start | bytes 1572872 | tf_op jit(solution)/shard_map/ppermute | solution.py:17
  708.4 119.9 %all-to-all-start.1 = ((bf16[64,8,128]{2,0,1:T(8,128)(2,1)}), bf16[64,8,128]{2,0,1:T(8,128)(2,1)S(1)}, u32[]{:S(2)}, u32[]{:S(2)}) async-start(bf16[64,8,128]{2,0,1:T(8,128)(2,1)} %copy_bitcast_fusion.2), calls=%async_computation.2 | async-start | bytes 262144 | tf_op jit(solution)/shard_map/all_to_all | solution.py:67
Sparse Core Ops, SparseCore 0:
  11.1 268.2 all-gather.13
  282.5 180.5 all-gather.11
  466.1 175.0 all-gather.9
  648.5 57.9 reduce-scatter.1
  710.6 112.8 all-gather.7
